TPU v7x, 256 devices: a whole 4x4x8 slice. The times are simulated.
256 devices in a mesh: series: 64 (over z_hi, y, x, core), tick: 4 (over z_lo).
Axes of the slice: x: 4, y: 4, z: 8 (z_hi: 2, z_lo: 4; z = z_hi * 4 + z_lo), core: 2. Of those that a mesh axis runs over, the one named last changes fastest.
Arguments:
- telemetry: float32 [32768, 1024], P('series', 'tick'), may hold values from -81 to 81
- sparse: float32 [32768, 1024], P('series', 'tick'), may hold values from -4 to 4
- multiplier: float32 [32768, 1024], P('series', 'tick'), may hold values from -4 to 4
Outputs:
- lowrank: float32 [32768, 1024], P('series', 'tick')
- new_sparse: float32 [32768, 1024], P('series', 'tick')
- new_multiplier: float32 [32768, 1024], P('series', 'tick')
All inputs are finite; a program needn't handle non-finite values.
Results may differ from a plain program's by a relative error of at most 0.0003.
Values sent between devices are 32-bit elements; how exact they have to be, the bound alone decides.
A program may use at most 64 MiB of HBM per device.

v0:
```python
import jax
import jax.numpy as jnp
from jax import lax
from jax.sharding import PartitionSpec as P

chebyshev_coefs = (0.4, 0.5, 0.1, -0.04, -0.06)
shrink_level = 0.5


def on_device(telemetry, sparse, multiplier):
    blended = telemetry - sparse + multiplier
    full_rows = lax.all_gather(blended, "tick", axis=1, tiled=True)
    partial_value = lax.dot_general(
        blended,
        full_rows,
        (((0,), (0,)), ((), ())),
        precision=lax.Precision.HIGHEST,
        preferred_element_type=jnp.float32,
    )
    gram_block = lax.psum(partial_value, "series")
    frobenius = jnp.sqrt(lax.psum(jnp.sum(gram_block * gram_block), "tick") + jnp.float32(1e-06))
    factor = 2.0 / frobenius
    first_image = lax.dot_general(
        full_rows,
        gram_block,
        (((1,), (1,)), ((), ())),
        precision=lax.Precision.HIGHEST,
        preferred_element_type=jnp.float32,
    )
    earlier = blended
    current = factor * first_image - blended
    lowrank = chebyshev_coefs[0] * earlier + chebyshev_coefs[1] * current
    for degree in range(2, 5):
        product = lax.dot_general(
            lax.all_gather(current, "tick", axis=1, tiled=True),
            gram_block,
            (((1,), (1,)), ((), ())),
            precision=lax.Precision.HIGHEST,
            preferred_element_type=jnp.float32,
        )
        following = 2.0 * (factor * product - current) - earlier
        lowrank = lowrank + chebyshev_coefs[degree] * following
        earlier, current = (current, following)
    level = telemetry - lowrank + multiplier
    new_sparse = jnp.sign(level) * jnp.maximum(jnp.abs(level) - shrink_level, 0.0)
    new_multiplier = multiplier + telemetry - lowrank - new_sparse
    return (lowrank, new_sparse, new_multiplier)


def solution(mesh):
    return jax.shard_map(
        on_device,
        mesh=mesh,
        in_specs=(P("series", "tick"), P("series", "tick"), P("series", "tick")),
        out_specs=(P("series", "tick"), P("series", "tick"), P("series", "tick")),
        check_vma=False,
    )
```

profile of v0, /device:TPU:1, one launch (start us, length us, event | category | flops | bytes accessed | tf_op | source)
XLA Modules:
  0.0 1039.1 jit_solution(32527726666708900)
XLA Ops:
  7.2 0.0 all-gather.5.cloned.1.call-start
  7.2 2.3 subtract_add_fusion
  9.5 0.0 all-gather.5.cloned.1.call-update
  9.5 0.0 copy-start.1
  9.5 0.0 all-reduce.2.cloned.1.call-start
  9.5 54.7 %all-gather.5.cloned.1.call-done = f32[512,1024]{1,0:T(8,128)} async-done(((f32[512,256]{1,0:T(8,128)}), f32[512,1024]{1,0:T(8,128)}) %all-gather.5.cloned.1.call-update) | async-done | bytes 2097168 | tf_op jit(solution)/shard_map/all_gather | solution.py:12
  64.3 4.6 fusion.12
  68.9 0.0 all-reduce.2.cloned.1.call-update
  68.9 0.0 all-gather.7.cloned.1.call-start
  69.0 782.8 %all-reduce.2.cloned.1.call-done = f32[256,1024]{1,0:T(8,128)} async-done(((f32[256,1024]{1,0:T(8,128)}), f32[256,1024]{1,0:T(8,128)}) %all-reduce.2.cloned.1.call-update) | async-done | bytes 1048592 | tf_op jit(solution)/shard_map/psum | solution.py:20
  851.8 2.1 multiply_reduce_fusion
  853.9 7.8 psum.15
  862.4 0.0 copy-done.1
  862.4 0.0 copy-start
  862.4 4.6 fusion.3
  867.0 0.0 all-gather.7.cloned.1.call-update
  867.0 0.0 copy-start.2
  867.0 0.0 all-gather.9.cloned.1.call-start
  867.1 51.7 %all-gather.7.cloned.1.call-done = f32[512,1024]{1,0:T(8,128)} async-done(((f32[512,256]{1,0:T(8,128)}), f32[512,1024]{1,0:T(8,128)}) %all-gather.7.cloned.1.call-update) | async-done | bytes 2097168 | tf_op jit(solution)/shard_map/all_gather | solution.py:35
  918.8 0.0 copy-done
  918.8 4.3 fusion.5
  923.1 0.0 all-gather.9.cloned.1.call-update
  923.1 0.0 copy-start.3
  923.2 0.0 copy-start.4
  923.2 0.0 all-gather.11.cloned.1.call-start
  923.2 49.9 %all-gather.9.cloned.1.call-done = f32[512,1024]{1,0:T(8,128)} async-done(((f32[512,256]{1,0:T(8,128)}), f32[512,1024]{1,0:T(8,128)}) %all-gather.9.cloned.1.call-update) | async-done | bytes 2097168 | tf_op jit(solution)/shard_map/all_gather | solution.py:35
  973.1 0.0 copy-done.2
  973.1 4.3 fusion.7
  977.4 0.0 all-gather.11.cloned.1.call-update
  977.4 49.9 %all-gather.11.cloned.1.call-done = f32[512,1024]{1,0:T(8,128)} async-done(((f32[512,256]{1,0:T(8,128)}), f32[512,1024]{1,0:T(8,128)}) %all-gather.11.cloned.1.call-update) | async-done | bytes 2097168 | tf_op jit(solution)/shard_map/all_gather | solution.py:35
  1027.4 0.0 copy-done.3
  1027.4 0.0 copy-done.4
  1027.4 5.2 subtract_subtract_fusion
Async XLA Ops:
  7.2 57.1 %all-gather.5.cloned.1.call-start = ((), (), s32[]{:S(2)}) async-start(), calls=%async_computation | async-start | bytes 2621440 | tf_op jit(solution)/shard_map/all_gather | solution.py:12
  9.5 852.9 %copy-start.1 = (f32[512,256]{1,0:T(8,128)S(1)}, f32[512,256]{1,0:T(8,128)}, u32[]{:S(2)}) copy-start(f32[512,256]{1,0:T(8,128)} %subtract_add_fusion) | copy-start | bytes 1572868
  9.5 842.3 %all-reduce.2.cloned.1.call-start = ((), (), s32[]{:S(2)}) async-start(), calls=%async_computation.1 | async-start | bytes 2097152 | tf_op jit(solution)/shard_map/psum | solution.py:20
  68.9 849.9 %all-gather.7.cloned.1.call-start = ((), (), s32[]{:S(2)}) async-start(), calls=%async_computation.2 | async-start | bytes 2621440 | tf_op jit(solution)/shard_map/all_gather | solution.py:35
  862.4 56.4 %copy-start = (f32[256,1024]{1,0:T(8,128)S(1)}, f32[256,1024]{1,0:T(8,128)}, u32[]{:S(2)}) copy-start(f32[256,1024]{1,0:T(8,128)} %all-reduce.2.cloned.1.call-done) | copy-start | bytes 3145732
  867.0 106.1 %copy-start.2 = (f32[512,256]{1,0:T(8,128)S(1)}, f32[512,256]{1,0:T(8,128)}, u32[]{:S(2)}) copy-start(f32[512,256]{1,0:T(8,128)} %fusion.3) | copy-start | bytes 1572868
  867.0 106.1 %all-gather.9.cloned.1.call-start = ((), (), s32[]{:S(2)}) async-start(), calls=%async_computation.3 | async-start | bytes 2621440 | tf_op jit(solution)/shard_map/all_gather | solution.py:35
  923.1 104.2 %copy-start.3 = (f32[512,256]{1,0:T(8,128)S(1)}, f32[512,256]{1,0:T(8,128)}, u32[]{:S(2)}) copy-start(f32[512,256]{1,0:T(8,128)} %fusion.5) | copy-start | bytes 1572868
  923.2 104.2 %copy-start.4 = (f32[512,256]{1,0:T(8,128)S(1)}, f32[512,256]{1,0:T(8,128)}, u32[]{:S(2)}) copy-start(f32[512,256]{1,0:T(8,128)} %param.5) | copy-start | bytes 1572868
  923.2 104.2 %all-gather.11.cloned.1.call-start = ((), (), s32[]{:S(2)}) async-start(), calls=%async_computation.4 | async-start | bytes 2621440 | tf_op jit(solution)/shard_map/all_gather | solution.py:35
Sparse Core Ops, SparseCore 0:
  10.4 53.8 all-gather.4
  69.0 782.7 all-reduce.1
  867.1 51.6 all-gather.6
  923.3 49.7 all-gather.8
  977.5 49.7 all-gather.10
where the time goes:
time: 1040 us
  waiting for transfers between devices  989 us (95%)
  matrix products  23 us (2%)
  between operations  14.5 us (1%)
    psum x1, waiting for transfers between devices, on_device(): gram_block = lax.psum(partial_value, 'series')  783 us
    all_gather x3, waiting for transfers between devices, on_device(): lax.all_gather(current, 'tick', axis=1, tiled=True)  152 us
    all_gather x1, waiting for transfers between devices, on_device(): full_rows = lax.all_gather(blended, 'tick', axis=1, tiled=True)  54.7 us
  transfers between devices with their start and end apart: 5, of which 5 were waited for; matrix products, arithmetic and copies ran while one was open for 0% of the time, Pallas kernels for 0%

commit v1 on v0

v1 whole, which is shorter than its diff:
```python
import functools

import jax
import jax.numpy as jnp
from jax import lax
from jax.experimental import pallas as pl
from jax.experimental.pallas import tpu as pltpu
from jax.sharding import PartitionSpec as P

MESH = pl.DeviceIdType.MESH
coefs = (0.4, 0.5, 0.1, -0.04, -0.06)
shrink_level = 0.5
f32, bf16 = jnp.float32, jnp.bfloat16

pairs = (
    ((0, 0), (0, 1), (0, 2), (0, 3), (1, 1)),
    ((1, 2), (1, 3), (2, 2), (2, 3), (3, 3)),
)


def split(value):
    high = value.astype(bf16)
    return high, (value - high.astype(f32)).astype(bf16)


def dot(a, b, dims=((1,), (0,))):
    return lax.dot_general(a, b, (dims, ((), ())), preferred_element_type=f32)


def kernel(
    tele, sparse, mult, low_out, sparse_out, mult_out,
    wf, wp, gh, gl, part, r1, s1, r2, s2, r3, g2, g1, gf,
    gc, gch, gcl, va, vb, vh, vl, acc, wfh, wfl, ss, rs,
):
    series, t = lax.axis_index("series"), lax.axis_index("tick")
    c = series % 2
    x = (series // 2) % 4
    y = (series // 8) % 4
    zh = series // 32

    def at(zh_, t_, y_, x_, c_):
        return ((zh_ * 4 + y_) * 4 + x_) * 2 + c_, t_

    def xpeer(d):
        return at(zh, t, y, (x + d) % 4, c)

    def ypeer(d):
        return at(zh, t, (y + d) % 4, x, c)

    def zpeer(dh, d):
        return at((zh + dh) % 2, (t + d) % 4, y, x, c)

    partner = at(zh, t, y, x, 1 - c)
    count = [0]

    def send(src, dst, device):
        k = count[0]
        count[0] += 1
        copy = pltpu.make_async_remote_copy(
            src_ref=src, dst_ref=dst, send_sem=ss.at[k], recv_sem=rs.at[k],
            device_id=device, device_id_type=MESH,
        )
        copy.start()
        return copy

    sent = []

    barrier = pltpu.get_barrier_semaphore()
    peers = [xpeer(d) for d in (1, 2, 3)] + [ypeer(d) for d in (1, 2, 3)]
    peers += [zpeer(dh, d) for dh in (0, 1) for d in range(4) if dh or d] + [partner]
    for p in peers:
        pl.semaphore_signal(barrier, inc=1, device_id=p, device_id_type=MESH)
    wf[t] = tele[...] - sparse[...] + mult[...]
    pl.semaphore_wait(barrier, len(peers))

    first = []
    for d in (1, 2, 3):
        q = (t + d) % 4
        block = wf.at[t, pl.ds(128 * q, 128)]
        first.append(send(block, block, zpeer(0, d)))
    mine = pl.ds(pl.multiple_of(128 * t, 128), 128)
    passed = [send(wf.at[t, mine], wp.at[t], partner)]
    for d in (1, 2, 3):
        first[d - 1].wait_recv()
        o = (t - d + 4) % 4
        passed.append(send(wf.at[o, mine], wp.at[o], partner))
    sent += first + passed

    rest = []
    for d in (1, 2, 3):
        q = (t + d) % 4
        for e in (1, 2, 3):
            block = wf.at[t, pl.ds(128 * ((q + e) % 4), 128)]
            rest.append(send(block, block, zpeer(0, d)))
    sent += rest

    for a in range(4):
        high, low = split(wf[a, mine])
        gh[a, 0:128] = high
        gl[a, 0:128] = low
    for copy in passed:
        copy.wait_recv()
    for a in range(4):
        high, low = split(wp[a])
        gh[a, 128:256] = high
        gl[a, 128:256] = low
    for k in range(5):
        (a0, b0), (a1, b1) = pairs[0][k], pairs[1][k]
        a, b = a0 + c * (a1 - a0), b0 + c * (b1 - b0)
        rows = ((0,), (0,))
        block = dot(gh[a], gh[b], rows) + (dot(gh[a], gl[b], rows) + dot(gl[a], gh[b], rows))
        part[0, 256 * k : 256 * k + 256] = block[:, :128]
        part[1, 256 * k : 256 * k + 256] = block[:, 128:]

    step = []
    for d in (1, 2, 3):
        step.append(send(part.at[0, pl.ds(320 * ((x + d) % 4), 320)], r1.at[0, d - 1], xpeer(d)))
        step.append(send(part.at[1, pl.ds(320 * ((y + d) % 4), 320)], r1.at[1, d - 1], ypeer(d)))
    for copy in step:
        copy.wait_recv()
    sent += step
    for h, i in ((0, x), (1, y)):
        own = part[h, pl.ds(pl.multiple_of(320 * i, 320), 320)]
        s1[h] = (own + r1[h, 0]) + (r1[h, 1] + r1[h, 2])

    step = []
    for d in (1, 2, 3):
        step.append(send(s1.at[0, pl.ds(80 * ((y + d) % 4), 80)], r2.at[0, d - 1], ypeer(d)))
        step.append(send(s1.at[1, pl.ds(80 * ((x + d) % 4), 80)], r2.at[1, d - 1], xpeer(d)))
    for copy in step:
        copy.wait_recv()
    sent += step
    for h, i in ((0, y), (1, x)):
        own = s1[h, pl.ds(pl.multiple_of(80 * i, 80), 80)]
        s2[80 * h : 80 * h + 80] = (own + r2[h, 0]) + (r2[h, 1] + r2[h, 2])

    step = []
    for dh in (0, 1):
        for d in range(4):
            if dh or d:
                step.append(send(s2.at[pl.ds(40 * ((t + d) % 4), 40)], r3.at[zh, t], zpeer(dh, d)))
    chunk = pl.ds(pl.multiple_of(40 * t, 40), 40)
    r3[zh, t] = s2[chunk]
    for copy in step:
        copy.wait_recv()
    sent += step
    total = r3[0, 0]
    for i in range(1, 8):
        total = total + r3[i // 4, i % 4]
    g2[chunk] = total

    step = []
    for d in (1, 2, 3):
        step.append(send(g2.at[chunk], g2.at[chunk], zpeer(0, d)))
    for copy in step:
        copy.wait_recv()
    sent += step
    step = []
    rows_y = pl.ds(pl.multiple_of(80 * y, 80), 80)
    rows_x = pl.ds(pl.multiple_of(80 * x, 80), 80)
    for d in (1, 2, 3):
        step.append(send(g2.at[pl.ds(0, 80)], g1.at[0, rows_y], ypeer(d)))
        step.append(send(g2.at[pl.ds(80, 80)], g1.at[1, rows_x], xpeer(d)))
    g1[0, rows_y] = g2[0:80]
    g1[1, rows_x] = g2[80:160]
    for copy in step:
        copy.wait_recv()
    sent += step
    step = []
    rows_x = pl.ds(pl.multiple_of(320 * x, 320), 320)
    rows_y = pl.ds(pl.multiple_of(320 * y, 320), 320)
    for d in (1, 2, 3):
        step.append(send(g1.at[0], gf.at[c, 0, rows_x], xpeer(d)))
        step.append(send(g1.at[1], gf.at[c, 1, rows_y], ypeer(d)))
    gf[c, 0, rows_x] = g1[0]
    gf[c, 1, rows_y] = g1[1]
    for copy in step:
        copy.wait_recv()
    sent += step
    swap = send(gf.at[c], gf.at[c], partner)
    sent.append(swap)
    swap.wait_recv()

    norm = jnp.zeros((1, 1), f32)
    for core in range(2):
        for k in range(5):
            a, b = pairs[core][k]
            block = jnp.concatenate(
                [gf[core, h, 256 * k : 256 * k + 256] for h in (0, 1)], axis=1
            )
            square = jnp.sum(jnp.sum(block * block, axis=0, keepdims=True), axis=1, keepdims=True)
            norm = norm + (square if a == b else 2.0 * square)
            high, low = split(block)
            gc[b, 256 * a : 256 * a + 256] = block
            gch[b, 256 * a : 256 * a + 256] = high
            gcl[b, 256 * a : 256 * a + 256] = low
            if a != b:
                block = block.T
                high, low = split(block)
                gc[a, 256 * b : 256 * b + 256] = block
                gch[a, 256 * b : 256 * b + 256] = high
                gcl[a, 256 * b : 256 * b + 256] = low
    factor = 2.0 / jnp.sqrt(norm + jnp.float32(1e-06))

    row = lax.broadcasted_iota(jnp.int32, (1024, 256), 0)
    col = lax.broadcasted_iota(jnp.int32, (1024, 256), 1)
    va[...] = jnp.where(row == col + 256 * t, 1.0, 0.0)
    vb[...] = factor * gc[t] - va[...]
    acc[...] = coefs[0] * va[...] + coefs[1] * vb[...]
    older, newer = va, vb
    for degree in (2, 3, 4):
        high, low = split(newer[...])
        vh[...] = high
        vl[...] = low
        for i in range(4):
            rows = slice(256 * i, 256 * i + 256)
            image = jnp.zeros((256, 256), f32)
            for k in range(4):
                kk = slice(256 * k, 256 * k + 256)
                image = image + (
                    dot(gch[k, rows], vh[kk])
                    + (dot(gch[k, rows], vl[kk]) + dot(gcl[k, rows], vh[kk]))
                )
            following = 2.0 * (factor * image - newer[rows]) - older[rows]
            acc[rows] = acc[rows] + coefs[degree] * following
            older[rows] = following
        older, newer = newer, older

    for copy in rest:
        copy.wait_recv()
    for a in range(4):
        high, low = split(wf[a])
        wfh[a] = high
        wfl[a] = low
    high, low = split(acc[...])
    vh[...] = high
    vl[...] = low
    for i in range(2):
        rows = slice(256 * i, 256 * i + 256)
        lowrank = jnp.zeros((256, 256), f32)
        for k in range(4):
            kk = slice(256 * k, 256 * k + 256)
            lowrank = lowrank + (
                dot(wfh[k, rows], vh[kk])
                + (dot(wfh[k, rows], vl[kk]) + dot(wfl[k, rows], vh[kk]))
            )
        level = tele[rows] - lowrank + mult[rows]
        size = jnp.maximum(jnp.abs(level) - shrink_level, 0.0)
        shrunk = jnp.where(level < 0.0, -size, size)
        low_out[rows] = lowrank
        sparse_out[rows] = shrunk
        mult_out[rows] = mult[rows] + tele[rows] - lowrank - shrunk
    for copy in sent:
        copy.wait_send()


copies = 3 + 4 + 9 + 6 + 6 + 7 + 3 + 6 + 6 + 1


def on_device(telemetry, sparse, multiplier):
    block = jax.ShapeDtypeStruct((512, 256), f32)
    vmem = pl.BlockSpec(memory_space=pltpu.VMEM)
    return pl.pallas_call(
        kernel,
        out_shape=(block, block, block),
        in_specs=[vmem] * 3,
        out_specs=(vmem, vmem, vmem),
        scratch_shapes=[
            pltpu.VMEM((4, 512, 256), f32),
            pltpu.VMEM((4, 128, 256), f32),
            pltpu.VMEM((4, 256, 256), bf16),
            pltpu.VMEM((4, 256, 256), bf16),
            pltpu.VMEM((2, 1280, 128), f32),
            pltpu.VMEM((2, 3, 320, 128), f32),
            pltpu.VMEM((2, 320, 128), f32),
            pltpu.VMEM((2, 3, 80, 128), f32),
            pltpu.VMEM((160, 128), f32),
            pltpu.VMEM((2, 4, 40, 128), f32),
            pltpu.VMEM((160, 128), f32),
            pltpu.VMEM((2, 320, 128), f32),
            pltpu.VMEM((2, 2, 1280, 128), f32),
            pltpu.VMEM((4, 1024, 256), f32),
            pltpu.VMEM((4, 1024, 256), bf16),
            pltpu.VMEM((4, 1024, 256), bf16),
            pltpu.VMEM((1024, 256), f32),
            pltpu.VMEM((1024, 256), f32),
            pltpu.VMEM((1024, 256), bf16),
            pltpu.VMEM((1024, 256), bf16),
            pltpu.VMEM((1024, 256), f32),
            pltpu.VMEM((4, 512, 256), bf16),
            pltpu.VMEM((4, 512, 256), bf16),
            pltpu.SemaphoreType.DMA((copies,)),
            pltpu.SemaphoreType.DMA((copies,)),
        ],
        compiler_params=pltpu.CompilerParams(
            collective_id=0, has_side_effects=True, vmem_limit_bytes=48 << 20
        ),
    )(telemetry, sparse, multiplier)


def solution(mesh):
    spec = P("series", "tick")
    return jax.shard_map(
        on_device,
        mesh=mesh,
        in_specs=(spec, spec, spec),
        out_specs=(spec, spec, spec),
        check_vma=False,
    )
```

time: 1040 us -> 96.3 us (0.09)
  waiting for transfers between devices: 989 us -> 0 us
  Pallas kernels: 0 us -> 89.9 us
  matrix products: 23 us -> 0 us
  between operations: 14.5 us -> 0.65 us
    psum x1 -> x0, waiting for transfers between devices: 783 us -> none  [on_device(): gram_block = lax.psum(partial_value, 'series')]
    all_gather x4 -> x0, waiting for transfers between devices: 206 us -> none  [the longest x3 152 us: on_device(): lax.all_gather(current, 'tick', axis=1, tiled=True)]
    pallas_call x0 -> x1, Pallas kernels: none -> 89.9 us  [on_device(): pl.pallas_call(kernel, out_shape=(block, block, block), in_specs=[vmem] *...]
    dot_general x5 -> x0, matrix products: 23 us -> none  [the longest x3 13.8 us: on_device(): lax.dot_general(lax.all_gather(current, 'tick', axis=1, tiled=True), gram...]
  transfers between devices with their start and end apart: 5 -> 0, of which waited for: 5 -> 0; matrix products, arithmetic and copies ran while one was open for 0% -> 0% of each run, Pallas kernels for 0% -> 0%
where the time goes in v1:
time: 96.3 us; the launch traced here: 96.1 us
  Pallas kernels  89.9 us (93%)
  local copies, waits for them, and re-layouts  5.5 us (6%)
    pallas_call x1, Pallas kernels, on_device(): pl.pallas_call(kernel, out_shape=(block, block, block), in_specs=[vmem] *...  89.9 us
    unnamed x9, local copies, waits for them, and re-layouts  5.5 us

profile of v1, /device:TPU:1, one launch (start us, length us, event | category | flops | bytes accessed | tf_op | source)
XLA Modules:
  0.0 96.1 jit_solution(10661716906599898083)
XLA Ops:
  0.6 0.0 copy-start
  0.6 1.0 %copy-done = f32[512,256]{1,0:T(8,128)S(1)} copy-done((f32[512,256]{1,0:T(8,128)S(1)}, f32[512,256]{1,0:T(8,128)}, u32[]{:S(2)}) %copy-start) | copy-done | bytes 524312
  1.7 0.0 copy-start.1
  1.7 1.0 %copy-done.1 = f32[512,256]{1,0:T(8,128)S(1)} copy-done((f32[512,256]{1,0:T(8,128)S(1)}, f32[512,256]{1,0:T(8,128)}, u32[]{:S(2)}) %copy-start.1) | copy-done | bytes 524312
  2.7 0.0 copy-start.2
  2.7 1.0 %copy-done.2 = f32[512,256]{1,0:T(8,128)S(1)} copy-done((f32[512,256]{1,0:T(8,128)S(1)}, f32[512,256]{1,0:T(8,128)}, u32[]{:S(2)}) %copy-start.2) | copy-done | bytes 524312
  3.8 89.9 %shard_map.58 = (f32[512,256]{1,0:T(8,128)S(1)}, f32[512,256]{1,0:T(8,128)S(1)}, f32[512,256]{1,0:T(8,128)S(1)}) custom-call(f32[512,256]{1,0:T(8,128)S(1)} %copy-done, f32[512,256]{1,0:T(8,128)S(1)} %copy-done.1, f32[512,256]{1,0:T(8,128)S(1)} %copy-done.2), custom_call_target="tpu_custom_call" | custom-call | tf_op jit(solution)/shard_map/pallas_call | solution.py:263
  93.7 0.8 copy.9
  94.5 0.8 copy.10
  95.3 0.8 copy.11
Async XLA Ops:
  0.6 1.0 %copy-start = (f32[512,256]{1,0:T(8,128)S(1)}, f32[512,256]{1,0:T(8,128)}, u32[]{:S(2)}) copy-start(f32[512,256]{1,0:T(8,128)} %tele.1) | copy-start | bytes 1572868
  1.7 1.0 %copy-start.1 = (f32[512,256]{1,0:T(8,128)S(1)}, f32[512,256]{1,0:T(8,128)}, u32[]{:S(2)}) copy-start(f32[512,256]{1,0:T(8,128)} %sparse.1) | copy-start | bytes 1572868
  2.7 1.0 %copy-start.2 = (f32[512,256]{1,0:T(8,128)S(1)}, f32[512,256]{1,0:T(8,128)}, u32[]{:S(2)}) copy-start(f32[512,256]{1,0:T(8,128)} %mult.1) | copy-start | bytes 1572868

commit v2 on v1

--- a/solution.py
+++ b/solution.py
@@ -28,9 +28,9 @@
 
 
 def kernel(
-    tele, sparse, mult, low_out, sparse_out, mult_out,
+    tele_in, sparse_in, mult_in, low_out, sparse_out, mult_out,
     wf, wp, gh, gl, part, r1, s1, r2, s2, r3, g2, g1, gf,
-    gc, gch, gcl, va, vb, vh, vl, acc, wfh, wfl, ss, rs,
+    gc, gch, gcl, va, vb, vh, vl, acc, wfh, wfl, tele, sparse, mult, ls, ss, rs,
 ):
     series, t = lax.axis_index("series"), lax.axis_index("tick")
     c = series % 2
@@ -64,12 +64,21 @@
         return copy
 
     sent = []
-
+    rest = []
+
+    loads = [
+        pltpu.make_async_copy(src, dst, ls.at[i])
+        for i, (src, dst) in enumerate(((tele_in, tele), (sparse_in, sparse), (mult_in, mult)))
+    ]
+    for load in loads:
+        load.start()
     barrier = pltpu.get_barrier_semaphore()
     peers = [xpeer(d) for d in (1, 2, 3)] + [ypeer(d) for d in (1, 2, 3)]
     peers += [zpeer(dh, d) for dh in (0, 1) for d in range(4) if dh or d] + [partner]
     for p in peers:
         pl.semaphore_signal(barrier, inc=1, device_id=p, device_id_type=MESH)
+    for load in loads:
+        load.wait()
     wf[t] = tele[...] - sparse[...] + mult[...]
     pl.semaphore_wait(barrier, len(peers))
 
@@ -86,13 +95,11 @@
         passed.append(send(wf.at[o, mine], wp.at[o], partner))
     sent += first + passed
 
-    rest = []
-    for d in (1, 2, 3):
-        q = (t + d) % 4
-        for e in (1, 2, 3):
+    def spread(kinds):
+        for d, e in kinds:
+            q = (t + d) % 4
             block = wf.at[t, pl.ds(128 * ((q + e) % 4), 128)]
             rest.append(send(block, block, zpeer(0, d)))
-    sent += rest
 
     for a in range(4):
         high, low = split(wf[a, mine])
@@ -112,6 +119,7 @@
         part[0, 256 * k : 256 * k + 256] = block[:, :128]
         part[1, 256 * k : 256 * k + 256] = block[:, 128:]
 
+    spread(((2, 1), (1, 1), (3, 1), (1, 2), (3, 2)))
     step = []
     for d in (1, 2, 3):
         step.append(send(part.at[0, pl.ds(320 * ((x + d) % 4), 320)], r1.at[0, d - 1], xpeer(d)))
@@ -155,6 +163,7 @@
     for copy in step:
         copy.wait_recv()
     sent += step
+    spread(((2, 2), (2, 3), (1, 3), (3, 3)))
     step = []
     rows_y = pl.ds(pl.multiple_of(80 * y, 80), 80)
     rows_x = pl.ds(pl.multiple_of(80 * x, 80), 80)
@@ -174,13 +183,18 @@
         step.append(send(g1.at[1], gf.at[c, 1, rows_y], ypeer(d)))
     gf[c, 0, rows_x] = g1[0]
     gf[c, 1, rows_y] = g1[1]
-    for copy in step:
-        copy.wait_recv()
-    sent += step
-    swap = send(gf.at[c], gf.at[c], partner)
-    sent.append(swap)
-    swap.wait_recv()
-
+    swap = []
+    for h, i in ((0, x), (1, y)):
+        piece = gf.at[c, h, pl.ds(320 * i, 320)]
+        swap.append(send(piece, piece, partner))
+    for d in (1, 2, 3):
+        for h, i in ((0, x), (1, y)):
+            step[2 * (d - 1) + h].wait_recv()
+            piece = gf.at[c, h, pl.ds(320 * ((i - d + 4) % 4), 320)]
+            swap.append(send(piece, piece, partner))
+    for copy in swap:
+        copy.wait_recv()
+    sent += step + swap
     norm = jnp.zeros((1, 1), f32)
     for core in range(2):
         for k in range(5):
@@ -250,11 +264,11 @@
         low_out[rows] = lowrank
         sparse_out[rows] = shrunk
         mult_out[rows] = mult[rows] + tele[rows] - lowrank - shrunk
-    for copy in sent:
+    for copy in sent + rest:
         copy.wait_send()
 
 
-copies = 3 + 4 + 9 + 6 + 6 + 7 + 3 + 6 + 6 + 1
+copies = 3 + 4 + 9 + 6 + 6 + 7 + 3 + 6 + 6 + 8
 
 
 def on_device(telemetry, sparse, multiplier):
@@ -263,7 +277,7 @@
     return pl.pallas_call(
         kernel,
         out_shape=(block, block, block),
-        in_specs=[vmem] * 3,
+        in_specs=[pl.BlockSpec(memory_space=pltpu.HBM)] * 3,
         out_specs=(vmem, vmem, vmem),
         scratch_shapes=[
             pltpu.VMEM((4, 512, 256), f32),
@@ -289,11 +303,15 @@
             pltpu.VMEM((1024, 256), f32),
             pltpu.VMEM((4, 512, 256), bf16),
             pltpu.VMEM((4, 512, 256), bf16),
+            pltpu.VMEM((512, 256), f32),
+            pltpu.VMEM((512, 256), f32),
+            pltpu.VMEM((512, 256), f32),
+            pltpu.SemaphoreType.DMA((3,)),
             pltpu.SemaphoreType.DMA((copies,)),
             pltpu.SemaphoreType.DMA((copies,)),
         ],
         compiler_params=pltpu.CompilerParams(
-            collective_id=0, has_side_effects=True, vmem_limit_bytes=48 << 20
+            collective_id=0, has_side_effects=True, vmem_limit_bytes=56 << 20
         ),
     )(telemetry, sparse, multiplier)
 

time: 96.3 us -> 78.4 us (0.81)
  Pallas kernels: 89.9 us -> 73.7 us
  local copies, waits for them, and re-layouts: 5.5 us -> 3.95 us
    pallas_call x1, Pallas kernels: 89.9 us -> 73.7 us  [on_device(): pl.pallas_call(kernel, out_shape=(block, block, block), in_specs=[pl.Bloc...]
    unnamed x9 -> x7, local copies, waits for them, and re-layouts: 5.5 us -> 3.95 us
where the time goes in v2:
time: 78.4 us; the launch traced here: 78.3 us
  Pallas kernels  73.7 us (94%)
  local copies, waits for them, and re-layouts  3.95 us (5%)
    pallas_call x1, Pallas kernels, on_device(): pl.pallas_call(kernel, out_shape=(block, block, block), in_specs=[pl.Bloc...  73.7 us
    unnamed x7, local copies, waits for them, and re-layouts  3.95 us

profile of v2, /device:TPU:1, one launch (start us, length us, event | category | flops | bytes accessed | tf_op | source)
XLA Modules:
  0.0 78.3 jit_solution(3690993150670887013)
XLA Ops:
  0.6 73.7 %shard_map.58 = (f32[512,256]{1,0:T(8,128)}, f32[512,256]{1,0:T(8,128)}, f32[512,256]{1,0:T(8,128)}) custom-call(f32[512,256]{1,0:T(8,128)} %tele_in.1, f32[512,256]{1,0:T(8,128)} %sparse_in.1, f32[512,256]{1,0:T(8,128)} %mult_in.1), custom_call_target="tpu_custom_call" | custom-call | tf_op jit(solution)/shard_map/pallas_call | solution.py:277
  74.3 0.0 copy-start.1
  74.3 1.9 %copy.9 = f32[512,256]{1,0:T(8,128)} copy(f32[512,256]{1,0:T(8,128)} %get-tuple-element.6) | data formatting | bytes 1048576
  76.2 0.0 copy-done.1
  76.2 0.0 copy-start
  76.2 0.8 %copy.10 = f32[512,256]{1,0:T(8,128)} copy(f32[512,256]{1,0:T(8,128)S(1)} %copy-done.1) | data formatting | bytes 1048576
  77.0 0.4 copy-done
  77.5 0.8 %copy.11 = f32[512,256]{1,0:T(8,128)} copy(f32[512,256]{1,0:T(8,128)S(1)} %copy-done) | data formatting | bytes 1048576
Async XLA Ops:
  74.3 1.9 %copy-start.1 = (f32[512,256]{1,0:T(8,128)S(1)}, f32[512,256]{1,0:T(8,128)}, u32[]{:S(2)}) copy-start(f32[512,256]{1,0:T(8,128)} %get-tuple-element.7) | copy-start | bytes 1572868
  76.2 1.2 %copy-start = (f32[512,256]{1,0:T(8,128)S(1)}, f32[512,256]{1,0:T(8,128)}, u32[]{:S(2)}) copy-start(f32[512,256]{1,0:T(8,128)} %get-tuple-element.8) | copy-start | bytes 1572868

commit v3 on v2

--- a/solution.py
+++ b/solution.py
@@ -28,8 +28,8 @@
 
 
 def kernel(
-    tele_in, sparse_in, mult_in, low_out, sparse_out, mult_out,
-    wf, wp, gh, gl, part, r1, s1, r2, s2, r3, g2, g1, gf,
+    tele_in, sparse_in, mult_in, low_out,
+    wf, wp, gh, gl, part, r1, s1, r2, s2, r3, g2, gf,
     gc, gch, gcl, va, vb, vh, vl, acc, wfh, wfl, tele, sparse, mult, ls, ss, rs,
 ):
     series, t = lax.axis_index("series"), lax.axis_index("tick")
@@ -53,14 +53,17 @@
     partner = at(zh, t, y, x, 1 - c)
     count = [0]
 
-    def send(src, dst, device):
+    def send(src, dst, device, here=None):
         k = count[0]
         count[0] += 1
         copy = pltpu.make_async_remote_copy(
             src_ref=src, dst_ref=dst, send_sem=ss.at[k], recv_sem=rs.at[k],
             device_id=device, device_id_type=MESH,
         )
-        copy.start()
+        if here is None:
+            copy.start()
+        else:
+            pl.when(here)(copy.start)
         return copy
 
     sent = []
@@ -95,11 +98,18 @@
         passed.append(send(wf.at[o, mine], wp.at[o], partner))
     sent += first + passed
 
-    def spread(kinds):
-        for d, e in kinds:
-            q = (t + d) % 4
-            block = wf.at[t, pl.ds(128 * ((q + e) % 4), 128)]
-            rest.append(send(block, block, zpeer(0, d)))
+    middle = (t - 1) * (t - 2) == 0
+    side = 1 - t // 2
+
+    def spread(d, e):
+        q = (t + d) % 4
+        block = wf.at[t, pl.ds(128 * ((q + e) % 4), 128)]
+        here, there = {1: (t != 3, t != 0), 2: (None, None), 3: (t != 0, t != 3)}[d]
+        rest.append((send(block, block, zpeer(0, d), here), here, there))
+
+    def relay(r):
+        block = wf.at[3 * side, pl.ds(128 * r, 128)]
+        rest.append((send(block, block, at(zh, 3 * (t // 2), y, x, c), middle), middle, (t - 1) * (t - 2) != 0))
 
     for a in range(4):
         high, low = split(wf[a, mine])
@@ -119,32 +129,43 @@
         part[0, 256 * k : 256 * k + 256] = block[:, :128]
         part[1, 256 * k : 256 * k + 256] = block[:, 128:]
 
-    spread(((2, 1), (1, 1), (3, 1), (1, 2), (3, 2)))
+    for k in (0, 1):
+        spread(2, (k + side) % 3 + 1)
+    relay(t)
+    spread(1, 1)
+    spread(3, 1)
+    def first_at(h, i, n):
+        return pl.ds(pl.multiple_of(320 * i + 80 * ((((y, x)[h]) + n) % 4), 80), 80)
+
+    order = (2, 1, 3)
+    step = {}
+    for n in order + (0,):
+        for d in order:
+            for h in (0, 1):
+                i, peer = ((x, xpeer), (y, ypeer))[h]
+                step[n, d, h] = send(part.at[h, first_at(h, (i + d) % 4, n)], r1.at[h, d - 1, n], peer(d))
+    step2 = {}
+    for n in order + (0,):
+        for h in (0, 1):
+            i, peer = ((x, ypeer), (y, xpeer))[h]
+            for d in order:
+                step[n, d, h].wait_recv()
+            value = (part[h, first_at(h, i, n)] + r1[h, 0, n]) + (r1[h, 1, n] + r1[h, 2, n])
+            if n:
+                s1[h, n - 1] = value
+                step2[n, h] = send(s1.at[h, n - 1], r2.at[h, n - 1], peer(n))
+            else:
+                s2[80 * h : 80 * h + 80] = value
+    sent += list(step.values()) + list(step2.values())
+    for h in (0, 1):
+        for n in order:
+            step2[n, h].wait_recv()
+        rows = slice(80 * h, 80 * h + 80)
+        s2[rows] = (s2[rows] + r2[h, 0]) + (r2[h, 1] + r2[h, 2])
+
     step = []
-    for d in (1, 2, 3):
-        step.append(send(part.at[0, pl.ds(320 * ((x + d) % 4), 320)], r1.at[0, d - 1], xpeer(d)))
-        step.append(send(part.at[1, pl.ds(320 * ((y + d) % 4), 320)], r1.at[1, d - 1], ypeer(d)))
-    for copy in step:
-        copy.wait_recv()
-    sent += step
-    for h, i in ((0, x), (1, y)):
-        own = part[h, pl.ds(pl.multiple_of(320 * i, 320), 320)]
-        s1[h] = (own + r1[h, 0]) + (r1[h, 1] + r1[h, 2])
-
-    step = []
-    for d in (1, 2, 3):
-        step.append(send(s1.at[0, pl.ds(80 * ((y + d) % 4), 80)], r2.at[0, d - 1], ypeer(d)))
-        step.append(send(s1.at[1, pl.ds(80 * ((x + d) % 4), 80)], r2.at[1, d - 1], xpeer(d)))
-    for copy in step:
-        copy.wait_recv()
-    sent += step
-    for h, i in ((0, y), (1, x)):
-        own = s1[h, pl.ds(pl.multiple_of(80 * i, 80), 80)]
-        s2[80 * h : 80 * h + 80] = (own + r2[h, 0]) + (r2[h, 1] + r2[h, 2])
-
-    step = []
-    for dh in (0, 1):
-        for d in range(4):
+    for dh in (1, 0):
+        for d in (0, 2, 1, 3):
             if dh or d:
                 step.append(send(s2.at[pl.ds(40 * ((t + d) % 4), 40)], r3.at[zh, t], zpeer(dh, d)))
     chunk = pl.ds(pl.multiple_of(40 * t, 40), 40)
@@ -163,38 +184,47 @@
     for copy in step:
         copy.wait_recv()
     sent += step
-    spread(((2, 2), (2, 3), (1, 3), (3, 3)))
-    step = []
-    rows_y = pl.ds(pl.multiple_of(80 * y, 80), 80)
-    rows_x = pl.ds(pl.multiple_of(80 * x, 80), 80)
-    for d in (1, 2, 3):
-        step.append(send(g2.at[pl.ds(0, 80)], g1.at[0, rows_y], ypeer(d)))
-        step.append(send(g2.at[pl.ds(80, 80)], g1.at[1, rows_x], xpeer(d)))
-    g1[0, rows_y] = g2[0:80]
-    g1[1, rows_x] = g2[80:160]
-    for copy in step:
-        copy.wait_recv()
-    sent += step
-    step = []
-    rows_x = pl.ds(pl.multiple_of(320 * x, 320), 320)
-    rows_y = pl.ds(pl.multiple_of(320 * y, 320), 320)
-    for d in (1, 2, 3):
-        step.append(send(g1.at[0], gf.at[c, 0, rows_x], xpeer(d)))
-        step.append(send(g1.at[1], gf.at[c, 1, rows_y], ypeer(d)))
-    gf[c, 0, rows_x] = g1[0]
-    gf[c, 1, rows_y] = g1[1]
-    swap = []
-    for h, i in ((0, x), (1, y)):
-        piece = gf.at[c, h, pl.ds(320 * i, 320)]
+    for k in (0, 1):
+        rest[k][0].wait_recv()
+        relay((2 * side + k) % 4)
+    spread(2, (2 + side) % 3 + 1)
+    for e in (2, 3):
+        spread(1, e)
+        spread(3, e)
+    def last_at(h, d, n):
+        own = (320 * ((x - d + 4) % 4) + 80 * ((y - n + 4) % 4), 320 * ((y - d + 4) % 4) + 80 * ((x - n + 4) % 4))[h]
+        return pl.ds(pl.multiple_of(own, 80), 80)
+
+    gathered, swap = {}, []
+
+    def onward(h, n):
+        piece = gf.at[c, h, last_at(h, 0, n)]
+        for d in order:
+            gathered[n, d, h] = send(piece, piece, (xpeer, ypeer)[h](d))
         swap.append(send(piece, piece, partner))
-    for d in (1, 2, 3):
-        for h, i in ((0, x), (1, y)):
-            step[2 * (d - 1) + h].wait_recv()
-            piece = gf.at[c, h, pl.ds(320 * ((i - d + 4) % 4), 320)]
-            swap.append(send(piece, piece, partner))
+
+    for h in (0, 1):
+        gf[c, h, last_at(h, 0, 0)] = g2[80 * h : 80 * h + 80]
+    step = {}
+    for d in order:
+        for h in (0, 1):
+            piece = gf.at[c, h, last_at(h, 0, 0)]
+            step[d, h] = send(piece, piece, (ypeer, xpeer)[h](d))
+    for h in (0, 1):
+        onward(h, 0)
+    for n in (1, 3, 2):
+        for h in (0, 1):
+            step[n, h].wait_recv()
+            onward(h, n)
+    for n in (0, 1, 3, 2):
+        for d in (1, 3, 2):
+            for h in (0, 1):
+                gathered[n, d, h].wait_recv()
+                piece = gf.at[c, h, last_at(h, d, n)]
+                swap.append(send(piece, piece, partner))
     for copy in swap:
         copy.wait_recv()
-    sent += step + swap
+    sent += list(step.values()) + list(gathered.values()) + swap
     norm = jnp.zeros((1, 1), f32)
     for core in range(2):
         for k in range(5):
@@ -240,8 +270,11 @@
             older[rows] = following
         older, newer = newer, older
 
-    for copy in rest:
-        copy.wait_recv()
+    for copy, _, there in rest[2:]:
+        if there is None:
+            copy.wait_recv()
+        else:
+            pl.when(there)(copy.wait_recv)
     for a in range(4):
         high, low = split(wf[a])
         wfh[a] = high
@@ -258,40 +291,39 @@
                 dot(wfh[k, rows], vh[kk])
                 + (dot(wfh[k, rows], vl[kk]) + dot(wfl[k, rows], vh[kk]))
             )
-        level = tele[rows] - lowrank + mult[rows]
-        size = jnp.maximum(jnp.abs(level) - shrink_level, 0.0)
-        shrunk = jnp.where(level < 0.0, -size, size)
-        low_out[rows] = lowrank
-        sparse_out[rows] = shrunk
-        mult_out[rows] = mult[rows] + tele[rows] - lowrank - shrunk
-    for copy in sent + rest:
+        low_out[rows] = 0.5 * lowrank
+    for copy in sent:
         copy.wait_send()
-
-
-copies = 3 + 4 + 9 + 6 + 6 + 7 + 3 + 6 + 6 + 8
+    for copy, here, _ in rest:
+        if here is None:
+            copy.wait_send()
+        else:
+            pl.when(here)(copy.wait_send)
+
+
+copies = 3 + 4 + 12 + 24 + 6 + 7 + 3 + 6 + 24 + 32
 
 
 def on_device(telemetry, sparse, multiplier):
     block = jax.ShapeDtypeStruct((512, 256), f32)
     vmem = pl.BlockSpec(memory_space=pltpu.VMEM)
-    return pl.pallas_call(
+    half = pl.pallas_call(
         kernel,
-        out_shape=(block, block, block),
+        out_shape=block,
         in_specs=[pl.BlockSpec(memory_space=pltpu.HBM)] * 3,
-        out_specs=(vmem, vmem, vmem),
+        out_specs=vmem,
         scratch_shapes=[
             pltpu.VMEM((4, 512, 256), f32),
             pltpu.VMEM((4, 128, 256), f32),
             pltpu.VMEM((4, 256, 256), bf16),
             pltpu.VMEM((4, 256, 256), bf16),
             pltpu.VMEM((2, 1280, 128), f32),
-            pltpu.VMEM((2, 3, 320, 128), f32),
-            pltpu.VMEM((2, 320, 128), f32),
+            pltpu.VMEM((2, 3, 4, 80, 128), f32),
+            pltpu.VMEM((2, 3, 80, 128), f32),
             pltpu.VMEM((2, 3, 80, 128), f32),
             pltpu.VMEM((160, 128), f32),
             pltpu.VMEM((2, 4, 40, 128), f32),
             pltpu.VMEM((160, 128), f32),
-            pltpu.VMEM((2, 320, 128), f32),
             pltpu.VMEM((2, 2, 1280, 128), f32),
             pltpu.VMEM((4, 1024, 256), f32),
             pltpu.VMEM((4, 1024, 256), bf16),
@@ -314,6 +346,11 @@
             collective_id=0, has_side_effects=True, vmem_limit_bytes=56 << 20
         ),
     )(telemetry, sparse, multiplier)
+    lowrank = 2.0 * half
+    level = telemetry - lowrank + multiplier
+    size = jnp.maximum(jnp.abs(level) - shrink_level, 0.0)
+    new_sparse = jnp.where(level < 0.0, -size, size)
+    return lowrank, new_sparse, multiplier + telemetry - lowrank - new_sparse
 
 
 def solution(mesh):

time: 78.4 us -> 73 us (0.931)
  local copies, waits for them, and re-layouts: 3.95 us -> 0.01 us
  Pallas kernels: 73.7 us -> 69.8 us
  other arithmetic: 0 us -> 2.36 us
    unnamed x7 -> x4, local copies, waits for them, and re-layouts: 3.95 us -> 0.01 us
    pallas_call x1, Pallas kernels: 73.7 us -> 69.8 us  [on_device(): pl.pallas_call(kernel, out_shape=block, in_specs=[pl.BlockSpec(memory_spa...]
    sub x0 -> x1, other arithmetic: none -> 2.36 us  [on_device(): return (lowrank, new_sparse, multiplier + telemetry - lowrank - new_sparse)]
where the time goes in v3:
time: 73 us; the launch traced here: 72.8 us
  Pallas kernels  69.8 us (96%)
  other arithmetic  2.36 us (3%)
    pallas_call x1, Pallas kernels, on_device(): pl.pallas_call(kernel, out_shape=block, in_specs=[pl.BlockSpec(memory_spa...  69.8 us
    sub x1, other arithmetic, on_device(): return (lowrank, new_sparse, multiplier + telemetry - lowrank - new_sparse)  2.36 us

profile of v3, /device:TPU:1, one launch (start us, length us, event | category | flops | bytes accessed | tf_op | source)
XLA Modules:
  0.0 72.8 jit_solution(117788956520889415)
XLA Ops:
  0.6 0.0 copy-start
  0.6 0.0 copy-start.1
  0.7 69.8 %shard_map.58 = f32[512,256]{1,0:T(8,128)} custom-call(f32[512,256]{1,0:T(8,128)} %tele_in.1, f32[512,256]{1,0:T(8,128)} %sparse_in.1, f32[512,256]{1,0:T(8,128)} %mult_in.1), custom_call_target="tpu_custom_call" | custom-call | tf_op jit(solution)/shard_map/pallas_call | solution.py:310
  70.4 0.0 copy-done
  70.4 0.0 copy-done.1
  70.4 2.4 %subtract_subtract_fusion = (f32[512,256]{1,0:T(8,128)}, f32[512,256]{1,0:T(8,128)}, f32[512,256]{1,0:T(8,128)}) fusion(f32[512,256]{1,0:T(8,128)S(1)} %copy-done, f32[512,256]{1,0:T(8,128)S(1)} %copy-done.1, f32[512,256]{1,0:T(8,128)} %shard_map.58), kind=kLoop, calls=%fused_computation.1 | loop fusion | flops 1572864 | bytes 3145728 | tf_op jit(solution)/shard_map/sub | solution.py:353
Async XLA Ops:
  0.6 69.8 %copy-start = (f32[512,256]{1,0:T(8,128)S(1)}, f32[512,256]{1,0:T(8,128)}, u32[]{:S(2)}) copy-start(f32[512,256]{1,0:T(8,128)} %mult_in.1) | copy-start | bytes 1572868
  0.6 69.8 %copy-start.1 = (f32[512,256]{1,0:T(8,128)S(1)}, f32[512,256]{1,0:T(8,128)}, u32[]{:S(2)}) copy-start(f32[512,256]{1,0:T(8,128)} %tele_in.1) | copy-start | bytes 1572868

commit v4 on v3

--- a/solution.py
+++ b/solution.py
@@ -12,10 +12,7 @@
 shrink_level = 0.5
 f32, bf16 = jnp.float32, jnp.bfloat16
 
-pairs = (
-    ((0, 0), (0, 1), (0, 2), (0, 3), (1, 1)),
-    ((1, 2), (1, 3), (2, 2), (2, 3), (3, 3)),
-)
+pairs = (((0, 1), (0, 2), (0, 3)), ((1, 2), (1, 3), (2, 3)))
 
 
 def split(value):
@@ -29,7 +26,7 @@
 
 def kernel(
     tele_in, sparse_in, mult_in, low_out,
-    wf, wp, gh, gl, part, r1, s1, r2, s2, r3, g2, gf,
+    wf, wp, dh, dl, dpart, dother, dr1, ds1, dr2, ds2, drz, gd, gh, gl, part, r1, s1, r2, s2, r3, g2, gf,
     gc, gch, gcl, va, vb, vh, vl, acc, wfh, wfl, tele, sparse, mult, ls, ss, rs,
 ):
     series, t = lax.axis_index("series"), lax.axis_index("tick")
@@ -67,7 +64,6 @@
         return copy
 
     sent = []
-    rest = []
 
     loads = [
         pltpu.make_async_copy(src, dst, ls.at[i])
@@ -90,26 +86,82 @@
         q = (t + d) % 4
         block = wf.at[t, pl.ds(128 * q, 128)]
         first.append(send(block, block, zpeer(0, d)))
+    middle = (t - 1) * (t - 2) == 0
+    ends = (t - 1) * (t - 2) != 0
+    side = 1 - t // 2
+    rest = []
+
+    def spread(d, e, early=None):
+        q = (t + d) % 4
+        block = wf.at[t, pl.ds(128 * ((q + e) % 4), 128)]
+        here, there = {1: (t != 3, t != 0), 2: (ends, middle), 3: (t != 0, t != 3)}[d]
+        copy = send(block, block, zpeer(0, d), here if early is None else early)
+        rest.append((copy, here, there))
+        return copy
+
+    def relay(o, r):
+        block = wf.at[o, pl.ds(128 * r, 128)]
+        rest.append((send(block, block, at(zh, 3 * (t // 2), y, x, c), middle), middle, ends))
+
+    near = [spread(1, 2, t % 2 == 0), spread(3, 1, t % 2 == 1)]
     mine = pl.ds(pl.multiple_of(128 * t, 128), 128)
     passed = [send(wf.at[t, mine], wp.at[t], partner)]
+
+    order = (2, 1, 3)
+    cols = ((0,), (0,))
+    high, low = split(wf[t])
+    dh[...] = high
+    dl[...] = low
+    block = dot(dh[...], dh[...], cols) + (dot(dh[...], dl[...], cols) + dot(dl[...], dh[...], cols))
+    for h in (0, 1):
+        dpart[h] = block[:, 128 * h : 128 * h + 128]
+    low_half = pl.ds(pl.multiple_of(128 * c, 128), 128)
+    high_half = pl.ds(pl.multiple_of(128 * (1 - c), 128), 128)
+    cross = send(dpart.at[:, high_half], dother, partner)
+    cross.wait_recv()
+    for h in (0, 1):
+        dother[h] = dpart[h, low_half] + dother[h]
+    step = {}
+    for d in order:
+        step[d, 0] = send(dother.at[0, pl.ds(32 * ((x + d) % 4), 32)], dr1.at[0, d - 1], xpeer(d))
+        step[d, 1] = send(dother.at[1, pl.ds(32 * ((y + d) % 4), 32)], dr1.at[1, d - 1], ypeer(d))
+    step2 = {}
+    for h, i in ((0, x), (1, y)):
+        for d in order:
+            step[d, h].wait_recv()
+        own = dother[h, pl.ds(pl.multiple_of(32 * i, 32), 32)]
+        ds1[h] = (own + dr1[h, 0]) + (dr1[h, 1] + dr1[h, 2])
+        i, peer = ((y, ypeer), (x, xpeer))[h]
+        for d in order:
+            step2[d, h] = send(ds1.at[h, pl.ds(8 * ((i + d) % 4), 8)], dr2.at[h, d - 1], peer(d))
+    sent += [cross] + list(step.values()) + list(step2.values())
+
     for d in (1, 2, 3):
         first[d - 1].wait_recv()
         o = (t - d + 4) % 4
         passed.append(send(wf.at[o, mine], wp.at[o], partner))
     sent += first + passed
-
-    middle = (t - 1) * (t - 2) == 0
-    side = 1 - t // 2
-
-    def spread(d, e):
-        q = (t + d) % 4
-        block = wf.at[t, pl.ds(128 * ((q + e) % 4), 128)]
-        here, there = {1: (t != 3, t != 0), 2: (None, None), 3: (t != 0, t != 3)}[d]
-        rest.append((send(block, block, zpeer(0, d), here), here, there))
-
-    def relay(r):
-        block = wf.at[3 * side, pl.ds(128 * r, 128)]
-        rest.append((send(block, block, at(zh, 3 * (t // 2), y, x, c), middle), middle, (t - 1) * (t - 2) != 0))
+    for h, i in ((0, y), (1, x)):
+        for d in order:
+            step2[d, h].wait_recv()
+        own = ds1[h, pl.ds(pl.multiple_of(8 * i, 8), 8)]
+        ds2[h] = (own + dr2[h, 0]) + (dr2[h, 1] + dr2[h, 2])
+
+    along = []
+    for flip in (1, 0):
+        for d in (0, 2, 1, 3):
+            if flip or d:
+                along.append(send(ds2, drz.at[zh, t], zpeer(flip, d)))
+    drz[zh, t] = ds2[...]
+    sent += along
+    pl.when(t == 1)(near[0].start)
+    pl.when(t == 2)(near[1].start)
+    relay(3 * side, t)
+    relay((3 - t) % 4, t)
+    for k in (0, 1):
+        spread(2, (k + side) % 3 + 1)
+    spread(1, 3)
+    spread(3, 2)
 
     for a in range(4):
         high, low = split(wf[a, mine])
@@ -121,7 +173,7 @@
         high, low = split(wp[a])
         gh[a, 128:256] = high
         gl[a, 128:256] = low
-    for k in range(5):
+    for k in range(3):
         (a0, b0), (a1, b1) = pairs[0][k], pairs[1][k]
         a, b = a0 + c * (a1 - a0), b0 + c * (b1 - b0)
         rows = ((0,), (0,))
@@ -129,15 +181,9 @@
         part[0, 256 * k : 256 * k + 256] = block[:, :128]
         part[1, 256 * k : 256 * k + 256] = block[:, 128:]
 
-    for k in (0, 1):
-        spread(2, (k + side) % 3 + 1)
-    relay(t)
-    spread(1, 1)
-    spread(3, 1)
     def first_at(h, i, n):
-        return pl.ds(pl.multiple_of(320 * i + 80 * ((((y, x)[h]) + n) % 4), 80), 80)
-
-    order = (2, 1, 3)
+        return pl.ds(pl.multiple_of(192 * i + 48 * ((((y, x)[h]) + n) % 4), 48), 48)
+
     step = {}
     for n in order + (0,):
         for d in order:
@@ -155,21 +201,38 @@
                 s1[h, n - 1] = value
                 step2[n, h] = send(s1.at[h, n - 1], r2.at[h, n - 1], peer(n))
             else:
-                s2[80 * h : 80 * h + 80] = value
+                s2[48 * h : 48 * h + 48] = value
     sent += list(step.values()) + list(step2.values())
+    for copy in along:
+        copy.wait_recv()
+    back = []
+    for h, i, peer in ((0, 4 * x + y, ypeer), (1, 4 * y + x, xpeer)):
+        for tick in range(4):
+            gd[c, h, i, tick] = drz[0, tick, h] + drz[1, tick, h]
+        for d in order:
+            back.append(send(gd.at[c, h, i], gd.at[c, h, i], peer(d)))
+    sent += back
     for h in (0, 1):
         for n in order:
             step2[n, h].wait_recv()
-        rows = slice(80 * h, 80 * h + 80)
+        rows = slice(48 * h, 48 * h + 48)
         s2[rows] = (s2[rows] + r2[h, 0]) + (r2[h, 1] + r2[h, 2])
 
     step = []
     for dh in (1, 0):
         for d in (0, 2, 1, 3):
             if dh or d:
-                step.append(send(s2.at[pl.ds(40 * ((t + d) % 4), 40)], r3.at[zh, t], zpeer(dh, d)))
-    chunk = pl.ds(pl.multiple_of(40 * t, 40), 40)
+                step.append(send(s2.at[pl.ds(24 * ((t + d) % 4), 24)], r3.at[zh, t], zpeer(dh, d)))
+    chunk = pl.ds(pl.multiple_of(24 * t, 24), 24)
     r3[zh, t] = s2[chunk]
+    for copy in back:
+        copy.wait_recv()
+    back = []
+    for h, i, peer in ((0, x, xpeer), (1, y, ypeer)):
+        row = gd.at[c, h, pl.ds(4 * i, 4)]
+        for d in order:
+            back.append(send(row, row, peer(d)))
+    sent += back
     for copy in step:
         copy.wait_recv()
     sent += step
@@ -184,16 +247,18 @@
     for copy in step:
         copy.wait_recv()
     sent += step
+    early = len(rest)
+    for copy, _, there in rest:
+        pl.when(there)(copy.wait_recv)
     for k in (0, 1):
-        rest[k][0].wait_recv()
-        relay((2 * side + k) % 4)
+        relay(3 * side, 2 * side + k)
+        relay((3 - t) % 4, 2 * side + k)
     spread(2, (2 + side) % 3 + 1)
-    for e in (2, 3):
-        spread(1, e)
-        spread(3, e)
+    spread(1, 1)
+    spread(3, 3)
     def last_at(h, d, n):
-        own = (320 * ((x - d + 4) % 4) + 80 * ((y - n + 4) % 4), 320 * ((y - d + 4) % 4) + 80 * ((x - n + 4) % 4))[h]
-        return pl.ds(pl.multiple_of(own, 80), 80)
+        own = (192 * ((x - d + 4) % 4) + 48 * ((y - n + 4) % 4), 192 * ((y - d + 4) % 4) + 48 * ((x - n + 4) % 4))[h]
+        return pl.ds(pl.multiple_of(own, 48), 48)
 
     gathered, swap = {}, []
 
@@ -204,7 +269,7 @@
         swap.append(send(piece, piece, partner))
 
     for h in (0, 1):
-        gf[c, h, last_at(h, 0, 0)] = g2[80 * h : 80 * h + 80]
+        gf[c, h, last_at(h, 0, 0)] = g2[48 * h : 48 * h + 48]
     step = {}
     for d in order:
         for h in (0, 1):
@@ -212,6 +277,9 @@
             step[d, h] = send(piece, piece, (ypeer, xpeer)[h](d))
     for h in (0, 1):
         onward(h, 0)
+    for copy in back:
+        copy.wait_recv()
+    swap.append(send(gd.at[c], gd.at[c], partner))
     for n in (1, 3, 2):
         for h in (0, 1):
             step[n, h].wait_recv()
@@ -226,24 +294,32 @@
         copy.wait_recv()
     sent += list(step.values()) + list(gathered.values()) + swap
     norm = jnp.zeros((1, 1), f32)
+    for tick in range(4):
+        for core in range(2):
+            rows = slice(256 * tick + 128 * core, 256 * tick + 128 * core + 128)
+            block = jnp.concatenate([gd[core, h, :, tick].reshape(128, 128) for h in (0, 1)], axis=1)
+            norm = norm + jnp.sum(jnp.sum(block * block, axis=0, keepdims=True), axis=1, keepdims=True)
+            high, low = split(block)
+            gc[tick, rows] = block
+            gch[tick, rows] = high
+            gcl[tick, rows] = low
     for core in range(2):
-        for k in range(5):
+        for k in range(3):
             a, b = pairs[core][k]
             block = jnp.concatenate(
                 [gf[core, h, 256 * k : 256 * k + 256] for h in (0, 1)], axis=1
             )
             square = jnp.sum(jnp.sum(block * block, axis=0, keepdims=True), axis=1, keepdims=True)
-            norm = norm + (square if a == b else 2.0 * square)
+            norm = norm + 2.0 * square
             high, low = split(block)
             gc[b, 256 * a : 256 * a + 256] = block
             gch[b, 256 * a : 256 * a + 256] = high
             gcl[b, 256 * a : 256 * a + 256] = low
-            if a != b:
-                block = block.T
-                high, low = split(block)
-                gc[a, 256 * b : 256 * b + 256] = block
-                gch[a, 256 * b : 256 * b + 256] = high
-                gcl[a, 256 * b : 256 * b + 256] = low
+            block = block.T
+            high, low = split(block)
+            gc[a, 256 * b : 256 * b + 256] = block
+            gch[a, 256 * b : 256 * b + 256] = high
+            gcl[a, 256 * b : 256 * b + 256] = low
     factor = 2.0 / jnp.sqrt(norm + jnp.float32(1e-06))
 
     row = lax.broadcasted_iota(jnp.int32, (1024, 256), 0)
@@ -270,11 +346,8 @@
             older[rows] = following
         older, newer = newer, older
 
-    for copy, _, there in rest[2:]:
-        if there is None:
-            copy.wait_recv()
-        else:
-            pl.when(there)(copy.wait_recv)
+    for copy, _, there in rest[early:]:
+        pl.when(there)(copy.wait_recv)
     for a in range(4):
         high, low = split(wf[a])
         wfh[a] = high
@@ -295,13 +368,10 @@
     for copy in sent:
         copy.wait_send()
     for copy, here, _ in rest:
-        if here is None:
-            copy.wait_send()
-        else:
-            pl.when(here)(copy.wait_send)
-
-
-copies = 3 + 4 + 12 + 24 + 6 + 7 + 3 + 6 + 24 + 32
+        pl.when(here)(copy.wait_send)
+
+
+copies = 1 + 6 + 6 + 7 + 6 + 6 + 1 + 3 + 4 + 15 + 24 + 6 + 7 + 3 + 6 + 24 + 32
 
 
 def on_device(telemetry, sparse, multiplier):
@@ -315,16 +385,26 @@
         scratch_shapes=[
             pltpu.VMEM((4, 512, 256), f32),
             pltpu.VMEM((4, 128, 256), f32),
+            pltpu.VMEM((512, 256), bf16),
+            pltpu.VMEM((512, 256), bf16),
+            pltpu.VMEM((2, 256, 128), f32),
+            pltpu.VMEM((2, 128, 128), f32),
+            pltpu.VMEM((2, 3, 32, 128), f32),
+            pltpu.VMEM((2, 32, 128), f32),
+            pltpu.VMEM((2, 3, 8, 128), f32),
+            pltpu.VMEM((2, 8, 128), f32),
+            pltpu.VMEM((2, 4, 2, 8, 128), f32),
+            pltpu.VMEM((2, 2, 16, 4, 8, 128), f32),
             pltpu.VMEM((4, 256, 256), bf16),
             pltpu.VMEM((4, 256, 256), bf16),
-            pltpu.VMEM((2, 1280, 128), f32),
-            pltpu.VMEM((2, 3, 4, 80, 128), f32),
-            pltpu.VMEM((2, 3, 80, 128), f32),
-            pltpu.VMEM((2, 3, 80, 128), f32),
-            pltpu.VMEM((160, 128), f32),
-            pltpu.VMEM((2, 4, 40, 128), f32),
-            pltpu.VMEM((160, 128), f32),
-            pltpu.VMEM((2, 2, 1280, 128), f32),
+            pltpu.VMEM((2, 768, 128), f32),
+            pltpu.VMEM((2, 3, 4, 48, 128), f32),
+            pltpu.VMEM((2, 3, 48, 128), f32),
+            pltpu.VMEM((2, 3, 48, 128), f32),
+            pltpu.VMEM((96, 128), f32),
+            pltpu.VMEM((2, 4, 24, 128), f32),
+            pltpu.VMEM((96, 128), f32),
+            pltpu.VMEM((2, 2, 768, 128), f32),
             pltpu.VMEM((4, 1024, 256), f32),
             pltpu.VMEM((4, 1024, 256), bf16),
             pltpu.VMEM((4, 1024, 256), bf16),

time: 73 us -> 67.5 us (0.925)
  Pallas kernels: 69.8 us -> 64.3 us
    pallas_call x1, Pallas kernels: 69.8 us -> 64.3 us  [on_device(): pl.pallas_call(kernel, out_shape=block, in_specs=[pl.BlockSpec(memory_spa...]
where the time goes in v4:
time: 67.5 us; the launch traced here: 67.3 us
  Pallas kernels  64.3 us (95%)
  other arithmetic  2.36 us (3%)
    pallas_call x1, Pallas kernels, on_device(): pl.pallas_call(kernel, out_shape=block, in_specs=[pl.BlockSpec(memory_spa...  64.3 us
    sub x1, other arithmetic, on_device(): return (lowrank, new_sparse, multiplier + telemetry - lowrank - new_sparse)  2.36 us

profile of v4, /device:TPU:1, one launch (start us, length us, event | category | flops | bytes accessed | tf_op | source)
XLA Modules:
  0.0 67.3 jit_solution(13173180129439755400)
XLA Ops:
  0.6 0.0 copy-start
  0.6 0.0 copy-start.1
  0.7 64.3 %shard_map.58 = f32[512,256]{1,0:T(8,128)} custom-call(f32[512,256]{1,0:T(8,128)} %tele_in.1, f32[512,256]{1,0:T(8,128)} %sparse_in.1, f32[512,256]{1,0:T(8,128)} %mult_in.1), custom_call_target="tpu_custom_call" | custom-call | tf_op jit(solution)/shard_map/pallas_call | solution.py:380
  64.9 0.0 copy-done
  64.9 0.0 copy-done.1
  64.9 2.4 %subtract_subtract_fusion = (f32[512,256]{1,0:T(8,128)}, f32[512,256]{1,0:T(8,128)}, f32[512,256]{1,0:T(8,128)}) fusion(f32[512,256]{1,0:T(8,128)S(1)} %copy-done, f32[512,256]{1,0:T(8,128)S(1)} %copy-done.1, f32[512,256]{1,0:T(8,128)} %shard_map.58), kind=kLoop, calls=%fused_computation.1 | loop fusion | flops 1572864 | bytes 3145728 | tf_op jit(solution)/shard_map/sub | solution.py:433
Async XLA Ops:
  0.6 64.3 %copy-start = (f32[512,256]{1,0:T(8,128)S(1)}, f32[512,256]{1,0:T(8,128)}, u32[]{:S(2)}) copy-start(f32[512,256]{1,0:T(8,128)} %mult_in.1) | copy-start | bytes 1572868
  0.6 64.3 %copy-start.1 = (f32[512,256]{1,0:T(8,128)S(1)}, f32[512,256]{1,0:T(8,128)}, u32[]{:S(2)}) copy-start(f32[512,256]{1,0:T(8,128)} %tele_in.1) | copy-start | bytes 1572868

commit v5 on v4

--- a/solution.py
+++ b/solution.py
@@ -266,7 +266,6 @@
         piece = gf.at[c, h, last_at(h, 0, n)]
         for d in order:
             gathered[n, d, h] = send(piece, piece, (xpeer, ypeer)[h](d))
-        swap.append(send(piece, piece, partner))
 
     for h in (0, 1):
         gf[c, h, last_at(h, 0, 0)] = g2[48 * h : 48 * h + 48]
@@ -284,12 +283,13 @@
         for h in (0, 1):
             step[n, h].wait_recv()
             onward(h, n)
-    for n in (0, 1, 3, 2):
-        for d in (1, 3, 2):
-            for h in (0, 1):
-                gathered[n, d, h].wait_recv()
-                piece = gf.at[c, h, last_at(h, d, n)]
-                swap.append(send(piece, piece, partner))
+    for d in (0, 1, 3, 2):
+        for h in (0, 1):
+            if d:
+                for n in (0, 1, 3, 2):
+                    gathered[n, d, h].wait_recv()
+            row = gf.at[c, h, pl.ds(192 * (((x, y)[h] - d + 4) % 4), 192)]
+            swap.append(send(row, row, partner))
     for copy in swap:
         copy.wait_recv()
     sent += list(step.values()) + list(gathered.values()) + swap
@@ -371,7 +371,7 @@
         pl.when(here)(copy.wait_send)
 
 
-copies = 1 + 6 + 6 + 7 + 6 + 6 + 1 + 3 + 4 + 15 + 24 + 6 + 7 + 3 + 6 + 24 + 32
+copies = 1 + 6 + 6 + 7 + 6 + 6 + 1 + 3 + 4 + 15 + 24 + 6 + 7 + 3 + 6 + 24 + 8
 
 
 def on_device(telemetry, sparse, multiplier):

time: 67.5 us -> 67.2 us (level)
  no operation moved by 1% of the time
where the time goes in v5:
time: 67.2 us; the launch traced here: 67 us
  Pallas kernels  64 us (95%)
  other arithmetic  2.36 us (4%)
    pallas_call x1, Pallas kernels, on_device(): pl.pallas_call(kernel, out_shape=block, in_specs=[pl.BlockSpec(memory_spa...  64 us
    sub x1, other arithmetic, on_device(): return (lowrank, new_sparse, multiplier + telemetry - lowrank - new_sparse)  2.36 us

profile of v5, /device:TPU:1, one launch (start us, length us, event | category | flops | bytes accessed | tf_op | source)
XLA Modules:
  0.0 67.0 jit_solution(2016838137171625551)
XLA Ops:
  0.6 0.0 copy-start
  0.6 0.0 copy-start.1
  0.7 64.0 %shard_map.58 = f32[512,256]{1,0:T(8,128)} custom-call(f32[512,256]{1,0:T(8,128)} %tele_in.1, f32[512,256]{1,0:T(8,128)} %sparse_in.1, f32[512,256]{1,0:T(8,128)} %mult_in.1), custom_call_target="tpu_custom_call" | custom-call | tf_op jit(solution)/shard_map/pallas_call | solution.py:380
  64.7 0.0 copy-done
  64.7 0.0 copy-done.1
  64.7 2.4 %subtract_subtract_fusion = (f32[512,256]{1,0:T(8,128)}, f32[512,256]{1,0:T(8,128)}, f32[512,256]{1,0:T(8,128)}) fusion(f32[512,256]{1,0:T(8,128)S(1)} %copy-done, f32[512,256]{1,0:T(8,128)S(1)} %copy-done.1, f32[512,256]{1,0:T(8,128)} %shard_map.58), kind=kLoop, calls=%fused_computation.1 | loop fusion | flops 1572864 | bytes 3145728 | tf_op jit(solution)/shard_map/sub | solution.py:433
Async XLA Ops:
  0.6 64.0 %copy-start = (f32[512,256]{1,0:T(8,128)S(1)}, f32[512,256]{1,0:T(8,128)}, u32[]{:S(2)}) copy-start(f32[512,256]{1,0:T(8,128)} %mult_in.1) | copy-start | bytes 1572868
  0.6 64.0 %copy-start.1 = (f32[512,256]{1,0:T(8,128)S(1)}, f32[512,256]{1,0:T(8,128)}, u32[]{:S(2)}) copy-start(f32[512,256]{1,0:T(8,128)} %tele_in.1) | copy-start | bytes 1572868

commit v6 on v5

--- a/solution.py
+++ b/solution.py
@@ -22,6 +22,10 @@
 
 def dot(a, b, dims=((1,), (0,))):
     return lax.dot_general(a, b, (dims, ((), ())), preferred_element_type=f32)
+
+
+def product(high, low, other_high, other_low):
+    return dot(high, other_high) + (dot(high, other_low) + dot(low, other_high))
 
 
 def kernel(
@@ -223,6 +227,9 @@
         for d in (0, 2, 1, 3):
             if dh or d:
                 step.append(send(s2.at[pl.ds(24 * ((t + d) % 4), 24)], r3.at[zh, t], zpeer(dh, d)))
+    third = [spread(1, 1, t % 2 == 0), spread(3, 3, t % 2 == 1)]
+    held = rest[-2:]
+    del rest[-2:]
     chunk = pl.ds(pl.multiple_of(24 * t, 24), 24)
     r3[zh, t] = s2[chunk]
     for copy in back:
@@ -254,8 +261,9 @@
         relay(3 * side, 2 * side + k)
         relay((3 - t) % 4, 2 * side + k)
     spread(2, (2 + side) % 3 + 1)
-    spread(1, 1)
-    spread(3, 3)
+    pl.when(t == 1)(third[0].start)
+    pl.when(t == 2)(third[1].start)
+    rest += held
     def last_at(h, d, n):
         own = (192 * ((x - d + 4) % 4) + 48 * ((y - n + 4) % 4), 192 * ((y - d + 4) % 4) + 48 * ((x - n + 4) % 4))[h]
         return pl.ds(pl.multiple_of(own, 48), 48)
@@ -301,8 +309,8 @@
             norm = norm + jnp.sum(jnp.sum(block * block, axis=0, keepdims=True), axis=1, keepdims=True)
             high, low = split(block)
             gc[tick, rows] = block
-            gch[tick, rows] = high
-            gcl[tick, rows] = low
+            gch[rows, 256 * tick : 256 * tick + 256] = high
+            gcl[rows, 256 * tick : 256 * tick + 256] = low
     for core in range(2):
         for k in range(3):
             a, b = pairs[core][k]
@@ -313,13 +321,13 @@
             norm = norm + 2.0 * square
             high, low = split(block)
             gc[b, 256 * a : 256 * a + 256] = block
-            gch[b, 256 * a : 256 * a + 256] = high
-            gcl[b, 256 * a : 256 * a + 256] = low
+            gch[256 * a : 256 * a + 256, 256 * b : 256 * b + 256] = high
+            gcl[256 * a : 256 * a + 256, 256 * b : 256 * b + 256] = low
             block = block.T
             high, low = split(block)
             gc[a, 256 * b : 256 * b + 256] = block
-            gch[a, 256 * b : 256 * b + 256] = high
-            gcl[a, 256 * b : 256 * b + 256] = low
+            gch[256 * b : 256 * b + 256, 256 * a : 256 * a + 256] = high
+            gcl[256 * b : 256 * b + 256, 256 * a : 256 * a + 256] = low
     factor = 2.0 / jnp.sqrt(norm + jnp.float32(1e-06))
 
     row = lax.broadcasted_iota(jnp.int32, (1024, 256), 0)
@@ -334,13 +342,7 @@
         vl[...] = low
         for i in range(4):
             rows = slice(256 * i, 256 * i + 256)
-            image = jnp.zeros((256, 256), f32)
-            for k in range(4):
-                kk = slice(256 * k, 256 * k + 256)
-                image = image + (
-                    dot(gch[k, rows], vh[kk])
-                    + (dot(gch[k, rows], vl[kk]) + dot(gcl[k, rows], vh[kk]))
-                )
+            image = product(gch[rows], gcl[rows], vh[...], vl[...])
             following = 2.0 * (factor * image - newer[rows]) - older[rows]
             acc[rows] = acc[rows] + coefs[degree] * following
             older[rows] = following
@@ -350,20 +352,14 @@
         pl.when(there)(copy.wait_recv)
     for a in range(4):
         high, low = split(wf[a])
-        wfh[a] = high
-        wfl[a] = low
+        wfh[:, 256 * a : 256 * a + 256] = high
+        wfl[:, 256 * a : 256 * a + 256] = low
     high, low = split(acc[...])
     vh[...] = high
     vl[...] = low
     for i in range(2):
         rows = slice(256 * i, 256 * i + 256)
-        lowrank = jnp.zeros((256, 256), f32)
-        for k in range(4):
-            kk = slice(256 * k, 256 * k + 256)
-            lowrank = lowrank + (
-                dot(wfh[k, rows], vh[kk])
-                + (dot(wfh[k, rows], vl[kk]) + dot(wfl[k, rows], vh[kk]))
-            )
+        lowrank = product(wfh[rows], wfl[rows], vh[...], vl[...])
         low_out[rows] = 0.5 * lowrank
     for copy in sent:
         copy.wait_send()
@@ -406,15 +402,15 @@
             pltpu.VMEM((96, 128), f32),
             pltpu.VMEM((2, 2, 768, 128), f32),
             pltpu.VMEM((4, 1024, 256), f32),
-            pltpu.VMEM((4, 1024, 256), bf16),
-            pltpu.VMEM((4, 1024, 256), bf16),
+            pltpu.VMEM((1024, 1024), bf16),
+            pltpu.VMEM((1024, 1024), bf16),
             pltpu.VMEM((1024, 256), f32),
             pltpu.VMEM((1024, 256), f32),
             pltpu.VMEM((1024, 256), bf16),
             pltpu.VMEM((1024, 256), bf16),
             pltpu.VMEM((1024, 256), f32),
-            pltpu.VMEM((4, 512, 256), bf16),
-            pltpu.VMEM((4, 512, 256), bf16),
+            pltpu.VMEM((512, 1024), bf16),
+            pltpu.VMEM((512, 1024), bf16),
             pltpu.VMEM((512, 256), f32),
             pltpu.VMEM((512, 256), f32),
             pltpu.VMEM((512, 256), f32),

time: 67.2 us -> 67.7 us (level)
  no operation moved by 1% of the time
where the time goes in v6:
time: 67.7 us; the launch traced here: 67.6 us
  Pallas kernels  64.5 us (95%)
  other arithmetic  2.36 us (3%)
    pallas_call x1, Pallas kernels, on_device(): pl.pallas_call(kernel, out_shape=block, in_specs=[pl.BlockSpec(memory_spa...  64.5 us
    sub x1, other arithmetic, on_device(): return (lowrank, new_sparse, multiplier + telemetry - lowrank - new_sparse)  2.36 us

profile of v6, /device:TPU:1, one launch (start us, length us, event | category | flops | bytes accessed | tf_op | source)
XLA Modules:
  0.0 67.6 jit_solution(5078439089734344482)
XLA Ops:
  0.6 0.0 copy-start
  0.6 0.0 copy-start.1
  0.7 64.5 %shard_map.58 = f32[512,256]{1,0:T(8,128)} custom-call(f32[512,256]{1,0:T(8,128)} %tele_in.1, f32[512,256]{1,0:T(8,128)} %sparse_in.1, f32[512,256]{1,0:T(8,128)} %mult_in.1), custom_call_target="tpu_custom_call" | custom-call | tf_op jit(solution)/shard_map/pallas_call | solution.py:376
  65.2 0.0 copy-done
  65.2 0.0 copy-done.1
  65.2 2.4 %subtract_subtract_fusion = (f32[512,256]{1,0:T(8,128)}, f32[512,256]{1,0:T(8,128)}, f32[512,256]{1,0:T(8,128)}) fusion(f32[512,256]{1,0:T(8,128)S(1)} %copy-done, f32[512,256]{1,0:T(8,128)S(1)} %copy-done.1, f32[512,256]{1,0:T(8,128)} %shard_map.58), kind=kLoop, calls=%fused_computation.1 | loop fusion | flops 1572864 | bytes 3145728 | tf_op jit(solution)/shard_map/sub | solution.py:429
Async XLA Ops:
  0.6 64.5 %copy-start = (f32[512,256]{1,0:T(8,128)S(1)}, f32[512,256]{1,0:T(8,128)}, u32[]{:S(2)}) copy-start(f32[512,256]{1,0:T(8,128)} %mult_in.1) | copy-start | bytes 1572868
  0.6 64.5 %copy-start.1 = (f32[512,256]{1,0:T(8,128)S(1)}, f32[512,256]{1,0:T(8,128)}, u32[]{:S(2)}) copy-start(f32[512,256]{1,0:T(8,128)} %tele_in.1) | copy-start | bytes 1572868
